TPU v7x, 256 devices: a whole 4x4x8 slice. The times are simulated.
256 devices in a mesh: grid: 16 (over z_hi, y, core), band: 16 (over x, z_lo).
Axes of the slice: x: 4, y: 4, z: 8 (z_hi: 2, z_lo: 4; z = z_hi * 4 + z_lo), core: 2. Of those that a mesh axis runs over, the one named last changes fastest.
Arguments:
- states: bfloat16 [24576, 32768], P('grid', 'band')
- applied: bfloat16 [24576, 32768], P('grid', 'band')
Outputs:
- gram_block: float32 [512, 32768], P('grid', 'band')
- projected: float32 [512, 32768], P('grid', 'band')
All inputs are finite; a program needn't handle non-finite values.
Results may differ from a plain program's by a relative error of at most 0.0003.
Values may be sent and summed in bfloat16 or wider, within the bound.
A program may use at most 64 MiB of HBM per device.

v0:
```python
import jax
import jax.numpy as jnp
from jax import lax
from jax.experimental import pallas as pl
from jax.experimental.pallas import tpu as pltpu
from jax.sharding import PartitionSpec as P

MESH = pl.DeviceIdType.MESH
GROUP = 256
STEPS = 2
N_BAND = 16
N_Y = 4
N_Z = 4
ROWS = 32
PIECES = 4
SPANS = ((0, 1024), (1024, 256), (1280, 256))
KINDS = 2
Z_PARTS = 2
LEVELS = 255.0
POWER = 31.25
LOG_LOW = -125.0 * 0.6931471805599453
TINY = 1e-37
Z_ROWS = ROWS // Z_PARTS


def kernel(
    x_ref, h_ref, gram_ref, proj_ref,
    own, group, group_t, part, from_core, from_y, away, code, from_z, unit, from_unit,
    own_sem, group_send, group_recv, core_send, core_recv, y_send, y_recv, z_send, z_recv, unit_send, unit_recv, go, all_sent,
):
    width = own.shape[1]
    piece = width // PIECES
    grid_at, band_at = lax.axis_index("grid"), lax.axis_index("band")
    half, y_at, core = grid_at // 8, lax.rem(grid_at // 2, N_Y), lax.rem(grid_at, 2)

    def band(by):
        return {"band": lax.rem(band_at + by + N_BAND, N_BAND)}

    def along_y(by):
        return {"grid": half * 8 + lax.rem(y_at + by, N_Y) * 2 + core}

    sibling = {"grid": grid_at + 1 - 2 * core}
    opposite = {"grid": lax.rem(grid_at + 8, 16)}

    pair = {"band": band_at + 1 - 2 * lax.rem(band_at, 2)}
    z_low = lax.rem(band_at, N_Z)
    column = []
    for up in range(2):
        for by in range(N_Z):
            if up or by:
                there = band_at - z_low + lax.rem(z_low + by, N_Z)
                column.append({"grid": lax.rem(grid_at + 8 * up, 16), "band": there})

    load = pltpu.make_async_copy(x_ref, own, own_sem)
    load.start()

    barrier = pltpu.get_barrier_semaphore()
    partners = [band(1), band(-1), band(2), band(-2), sibling] + column
    partners += [along_y(k) for k in range(1, N_Y)]
    for partner in partners:
        pl.semaphore_signal(barrier, inc=1, device_id=partner, device_id_type=MESH)
    pl.semaphore_wait(barrier, len(partners))

    def group_copy(chunk, span):
        step = (1 - half) if chunk < KINDS else half
        source = x_ref if chunk % KINDS == 0 else h_ref
        low = pl.multiple_of(step * GROUP, GROUP)
        points = pl.ds(*SPANS[span])
        return pltpu.make_async_remote_copy(
            src_ref=source.at[points, pl.ds(low, GROUP)],
            dst_ref=group.at[chunk, points],
            send_sem=group_send.at[chunk, span],
            recv_sem=group_recv.at[chunk, span],
            device_id={"band": lax.rem(band_at + step + 1, N_BAND)},
            device_id_type=MESH,
        )

    def core_copy(chunk, p):
        cols = pl.ds(p * piece, piece)
        return pltpu.make_async_remote_copy(
            src_ref=part.at[chunk, 1 - core, :, :, cols],
            dst_ref=from_core.at[chunk, :, :, cols],
            send_sem=core_send.at[chunk, p],
            recv_sem=core_recv.at[chunk, p],
            device_id=sibling,
            device_id_type=MESH,
        )

    def y_copy(chunk, p, by):
        cols = pl.ds(p * piece, piece)
        return pltpu.make_async_remote_copy(
            src_ref=part.at[chunk, core, lax.rem(y_at + by, N_Y), :, cols],
            dst_ref=from_y.at[chunk, by - 1, :, cols],
            send_sem=y_send.at[chunk, p, by - 1],
            recv_sem=y_recv.at[chunk, p, by - 1],
            device_id=along_y(by),
            device_id_type=MESH,
        )

    def z_copy(kind, part_at):
        rows = pl.ds(part_at * Z_ROWS, Z_ROWS)
        return pltpu.make_async_remote_copy(
            src_ref=code.at[kind, rows],
            dst_ref=from_z.at[kind, rows],
            send_sem=z_send.at[kind, part_at],
            recv_sem=z_recv.at[kind, part_at],
            device_id=opposite,
            device_id_type=MESH,
        )

    def unit_copy():
        return pltpu.make_async_remote_copy(
            src_ref=unit,
            dst_ref=from_unit,
            send_sem=unit_send,
            recv_sem=unit_recv,
            device_id=opposite,
            device_id_type=MESH,
        )

    def encode(kind):
        largest = jnp.max(jnp.abs(away[kind]), axis=(0, 1), keepdims=True)
        sixteenth = jnp.maximum(largest * 0.0625, TINY)
        unit[kind] = jnp.broadcast_to(sixteenth, unit.shape[1:])
        inverse = 1.0 / sixteenth
        for p in range(PIECES):
            cols = pl.ds(p * piece, piece)
            value = away[kind, :, cols]
            level = jnp.abs(value) * 0.0625 * inverse
            size = jnp.exp(POWER * jnp.log(1.0 + LEVELS * level) + LOG_LOW)
            code[kind, :, cols] = jnp.where(value < 0, -size, size).astype(jnp.bfloat16)

    def decode(kind, rows, cols):
        got = from_z[kind, rows, cols].astype(jnp.float32)
        level = (jnp.exp((jnp.log(jnp.abs(got)) - LOG_LOW) * (1.0 / POWER)) - 1.0) * (1.0 / LEVELS)
        size = level * (from_unit[kind, 0:1, 0:1] * 16.0)
        return jnp.where(got < 0, -size, size)

    def transpose(chunk, span):
        points = pl.ds(*SPANS[span])
        group_copy(chunk, span).wait_recv()
        group_t[:, points] = group[chunk, points].T

    def multiply(chunk, p, points, add):
        cols = pl.ds(p * piece, piece)
        product = jnp.dot(
            group_t[:, points], own[points, cols], preferred_element_type=jnp.float32
        )
        for y in range(N_Y):
            for c in range(2):
                low = (2 * y + c) * ROWS
                rows = product[low : low + ROWS]
                part[chunk, c, y, :, cols] = part[chunk, c, y, :, cols] + rows if add else rows

    def pair_sum(chunk, p):
        cols = pl.ds(p * piece, piece)
        core_copy(chunk, p).wait_recv()
        part[chunk, core, :, :, cols] = part[chunk, core, :, :, cols] + from_core[chunk, :, :, cols]
        for by in (2, 1, 3):
            y_copy(chunk, p, by).start()

    def send_pieces(chunk, points, add):
        for p in range(PIECES):
            multiply(chunk, p, points, add)
            core_copy(chunk, p).start()
            if p > 0:
                pair_sum(chunk, p - 1)
        pair_sum(chunk, PIECES - 1)

    def products(chunk):
        for span in range(len(SPANS)):
            transpose(chunk, span)
        send_pieces(chunk, pl.ds(0, own.shape[0]), False)

    def first_products(chunk):
        transpose(chunk, 0)
        transpose(chunk, 1)
        for p in range(PIECES):
            multiply(chunk, p, pl.ds(0, SPANS[2][0]), False)

    def last_products(chunk):
        transpose(chunk, 2)
        send_pieces(chunk, pl.ds(*SPANS[2]), True)

    def y_sum(chunk, p):
        cols = pl.ds(p * piece, piece)
        for by in range(1, N_Y):
            y_copy(chunk, p, by).wait_recv()
        return (
            part[chunk, core, y_at, :, cols]
            + from_y[chunk, 0, :, cols]
            + from_y[chunk, 1, :, cols]
            + from_y[chunk, 2, :, cols]
        )

    def away_sum(chunk):
        for p in range(PIECES):
            away[chunk, :, pl.ds(p * piece, piece)] = y_sum(chunk, p)
        encode(chunk)

    def home_sum(chunk, out_ref):
        for p in range(PIECES):
            out_ref[:, pl.ds(p * piece, piece)] = y_sum(chunk, p)

    def finish(kind, out_ref):
        if kind == 0:
            unit_copy().wait_recv()
        for part_at in range(Z_PARTS):
            rows = pl.ds(part_at * Z_ROWS, Z_ROWS)
            z_copy(kind, part_at).wait_recv()
            for p in range(PIECES):
                cols = pl.ds(p * piece, piece)
                out_ref[rows, cols] += decode(kind, rows, cols)

    def start(chunk):
        for span in range(len(SPANS)):
            group_copy(chunk, span).start()

    def sent(chunk):
        for span in range(len(SPANS)):
            group_copy(chunk, span).wait_send()

    start(0)
    start(1)
    load.wait()
    products(0)
    sent(0)
    sent(1)
    pl.semaphore_signal(go, inc=1, device_id=pair, device_id_type=MESH)
    late = jnp.logical_or(
        jnp.logical_and(half == 0, z_low == N_Z - 1), jnp.logical_and(half == 1, z_low == 0)
    )
    @pl.when(late)
    def _():
        pl.semaphore_wait(go, 1)
    start(2)
    start(3)
    products(1)
    away_sum(0)
    away_sum(1)
    @pl.when(jnp.logical_not(late))
    def _():
        pl.semaphore_wait(go, 1)
    products(2)
    first_products(3)
    sent(2)
    sent(3)
    for there in column:
        pl.semaphore_signal(all_sent, inc=1, device_id=there, device_id_type=MESH)
    last_products(3)
    pl.semaphore_wait(all_sent, len(column))
    unit_copy().start()
    z_copy(0, 0).start()
    z_copy(0, 1).start()
    z_copy(1, 0).start()
    z_copy(1, 1).start()
    home_sum(2, gram_ref)
    home_sum(3, proj_ref)
    finish(0, gram_ref)
    finish(1, proj_ref)

    for chunk in range(KINDS * STEPS):
        for p in range(PIECES):
            core_copy(chunk, p).wait_send()
            for by in range(1, N_Y):
                y_copy(chunk, p, by).wait_send()
    unit_copy().wait_send()
    for kind in range(KINDS):
        for part_at in range(Z_PARTS):
            z_copy(kind, part_at).wait_send()


def per_device(states, applied):
    points, width = states.shape
    chunks = KINDS * STEPS
    f32, bf16, dma = jnp.float32, jnp.bfloat16, pltpu.SemaphoreType.DMA
    out = jax.ShapeDtypeStruct((ROWS, width), f32)
    return pl.pallas_call(
        kernel,
        out_shape=(out, out),
        in_specs=[pl.BlockSpec(memory_space=pl.ANY)] * 2,
        out_specs=(pl.BlockSpec(memory_space=pltpu.VMEM),) * 2,
        scratch_shapes=[
            pltpu.VMEM((points, width), bf16),
            pltpu.VMEM((chunks, points, GROUP), bf16),
            pltpu.VMEM((GROUP, points), bf16),
            pltpu.VMEM((chunks, 2, N_Y, ROWS, width), f32),
            pltpu.VMEM((chunks, N_Y, ROWS, width), f32),
            pltpu.VMEM((chunks, N_Y - 1, ROWS, width), f32),
            pltpu.VMEM((KINDS, ROWS, width), f32),
            pltpu.VMEM((KINDS, ROWS, width), bf16),
            pltpu.VMEM((KINDS, ROWS, width), bf16),
            pltpu.VMEM((KINDS, 8, 128), f32),
            pltpu.VMEM((KINDS, 8, 128), f32),
            dma,
            dma((chunks, len(SPANS))),
            dma((chunks, len(SPANS))),
            dma((chunks, PIECES)),
            dma((chunks, PIECES)),
            dma((chunks, PIECES, N_Y - 1)),
            dma((chunks, PIECES, N_Y - 1)),
            dma((KINDS, Z_PARTS)),
            dma((KINDS, Z_PARTS)),
            dma,
            dma,
            pltpu.SemaphoreType.REGULAR,
            pltpu.SemaphoreType.REGULAR,
        ],
        cost_estimate=pl.CostEstimate(
            flops=2 * points * width * GROUP * chunks, bytes_accessed=4 * points * width, transcendentals=0
        ),
        compiler_params=pltpu.CompilerParams(
            collective_id=0, has_side_effects=True, vmem_limit_bytes=48 * 2**20
        ),
        name="ritz_blocks",
    )(states, applied)


def solution(mesh):
    in_specs = (P("grid", "band"), P("grid", "band"))
    out_specs = (P("grid", "band"), P("grid", "band"))
    return jax.shard_map(
        per_device, mesh=mesh, in_specs=in_specs, out_specs=out_specs, check_vma=False
    )
```

profile of v0, /device:TPU:1, one launch (start us, length us, event | category | flops | bytes accessed | tf_op | source)
XLA Modules:
  0.0 135.8 jit_solution(6942564772575108266)
XLA Ops:
  0.6 133.8 %ritz_blocks.1 = (f32[32,2048]{1,0:T(8,128)S(1)}, f32[32,2048]{1,0:T(8,128)S(1)}) custom-call(bf16[1536,2048]{1,0:T(8,128)(2,1)} %x_ref.1, bf16[1536,2048]{1,0:T(8,128)(2,1)} %h_ref.1), custom_call_target="tpu_custom_call" | custom-call | flops 6442450944 | bytes 12582912 | tf_op jit(solution)/shard_map/ritz_blocks/pallas_call | solution.py:278
  134.4 0.7 copy.6
  135.1 0.7 copy.7
where the time goes:
time: 136 us
  Pallas kernels  134 us (99%)
  local copies, waits for them, and re-layouts  1.41 us (1%)
    pallas_call x1, Pallas kernels, per_device(): pl.pallas_call(kernel, out_shape=(out, out), in_specs=[pl.BlockSpec(memor...  134 us

commit v1 on v0

--- a/solution.py
+++ b/solution.py
@@ -12,7 +12,7 @@
 N_Y = 4
 N_Z = 4
 ROWS = 32
-PIECES = 4
+PIECES = 2
 SPANS = ((0, 1024), (1024, 256), (1280, 256))
 KINDS = 2
 Z_PARTS = 2
@@ -26,7 +26,7 @@
 def kernel(
     x_ref, h_ref, gram_ref, proj_ref,
     own, group, group_t, part, from_core, from_y, away, code, from_z, unit, from_unit,
-    own_sem, group_send, group_recv, core_send, core_recv, y_send, y_recv, z_send, z_recv, unit_send, unit_recv, go, all_sent,
+    own_sem, group_send, group_recv, core_send, core_recv, y_send, y_recv, z_send, z_recv, unit_send, unit_recv, go, go_on, all_sent,
 ):
     width = own.shape[1]
     piece = width // PIECES
@@ -42,7 +42,8 @@
     sibling = {"grid": grid_at + 1 - 2 * core}
     opposite = {"grid": lax.rem(grid_at + 8, 16)}
 
-    pair = {"band": band_at + 1 - 2 * lax.rem(band_at, 2)}
+    beside = band_at + 1 - 2 * lax.rem(band_at, 2)
+    pair = [{"grid": grid_at, "band": beside}, {"grid": sibling["grid"], "band": beside}]
     z_low = lax.rem(band_at, N_Z)
     column = []
     for up in range(2):
@@ -55,7 +56,7 @@
     load.start()
 
     barrier = pltpu.get_barrier_semaphore()
-    partners = [band(1), band(-1), band(2), band(-2), sibling] + column
+    partners = [band(1), band(-1), band(2), band(-2), sibling] + pair + column
     partners += [along_y(k) for k in range(1, N_Y)]
     for partner in partners:
         pl.semaphore_signal(barrier, inc=1, device_id=partner, device_id_type=MESH)
@@ -225,22 +226,33 @@
     load.wait()
     products(0)
     sent(0)
-    sent(1)
-    pl.semaphore_signal(go, inc=1, device_id=pair, device_id_type=MESH)
+    group_copy(1, 0).wait_send()
+    group_copy(1, 1).wait_send()
+    for there in pair:
+        pl.semaphore_signal(go, inc=1, device_id=there, device_id_type=MESH)
+    group_copy(1, 2).wait_send()
+    for there in pair:
+        pl.semaphore_signal(go_on, inc=1, device_id=there, device_id_type=MESH)
     late = jnp.logical_or(
         jnp.logical_and(half == 0, z_low == N_Z - 1), jnp.logical_and(half == 1, z_low == 0)
     )
     @pl.when(late)
     def _():
-        pl.semaphore_wait(go, 1)
-    start(2)
+        pl.semaphore_wait(go, 2)
+    group_copy(2, 2).start()
+    @pl.when(late)
+    def _():
+        pl.semaphore_wait(go_on, 2)
+    group_copy(2, 0).start()
+    group_copy(2, 1).start()
     start(3)
     products(1)
     away_sum(0)
     away_sum(1)
     @pl.when(jnp.logical_not(late))
     def _():
-        pl.semaphore_wait(go, 1)
+        pl.semaphore_wait(go, 2)
+        pl.semaphore_wait(go_on, 2)
     products(2)
     first_products(3)
     sent(2)
@@ -248,13 +260,13 @@
     for there in column:
         pl.semaphore_signal(all_sent, inc=1, device_id=there, device_id_type=MESH)
     last_products(3)
+    home_sum(2, gram_ref)
     pl.semaphore_wait(all_sent, len(column))
     unit_copy().start()
     z_copy(0, 0).start()
     z_copy(0, 1).start()
     z_copy(1, 0).start()
     z_copy(1, 1).start()
-    home_sum(2, gram_ref)
     home_sum(3, proj_ref)
     finish(0, gram_ref)
     finish(1, proj_ref)
@@ -305,6 +317,7 @@
             dma,
             pltpu.SemaphoreType.REGULAR,
             pltpu.SemaphoreType.REGULAR,
+            pltpu.SemaphoreType.REGULAR,
         ],
         cost_estimate=pl.CostEstimate(
             flops=2 * points * width * GROUP * chunks, bytes_accessed=4 * points * width, transcendentals=0

time: 136 us -> 135 us (level)
  no operation moved by 1% of the time
where the time goes in v1:
time: 135 us
  Pallas kernels  133 us (99%)
  local copies, waits for them, and re-layouts  1.41 us (1%)
    pallas_call x1, Pallas kernels, per_device(): pl.pallas_call(kernel, out_shape=(out, out), in_specs=[pl.BlockSpec(memor...  133 us

profile of v1, /device:TPU:1, one launch (start us, length us, event | category | flops | bytes accessed | tf_op | source)
XLA Modules:
  0.0 135.2 jit_solution(11538679288513687551)
XLA Ops:
  0.6 133.2 %ritz_blocks.1 = (f32[32,2048]{1,0:T(8,128)S(1)}, f32[32,2048]{1,0:T(8,128)S(1)}) custom-call(bf16[1536,2048]{1,0:T(8,128)(2,1)} %x_ref.1, bf16[1536,2048]{1,0:T(8,128)(2,1)} %h_ref.1), custom_call_target="tpu_custom_call" | custom-call | flops 6442450944 | bytes 12582912 | tf_op jit(solution)/shard_map/ritz_blocks/pallas_call | solution.py:290
  133.8 0.7 copy.6
  134.5 0.7 copy.7
